TPU v7x, 128 devices: a whole 4x4x4 slice. The times are simulated.
128 devices in a mesh: chain: 128 (over z, y, x, core).
Axes of the slice: x: 4, y: 4, z: 4, core: 2. Of those that a mesh axis runs over, the one named last changes fastest.
Arguments:
- sketch: float32 [256, 64, 256], P('chain'), may hold values from -42 to 42
- inv_diag: float32 [256, 256, 256], P('chain'), may hold values from -0.1 to 1.5
- upper: float32 [256, 256, 256], P('chain'), may hold values from -1.5 to 1.5
- lower: float32 [256, 256, 256], P('chain'), may hold values from -1.1 to 1.1
Outputs:
- basis: float32 [256, 64, 256], P('chain')
- r_factor: float32 [64, 64], replicated
All inputs are finite; a program needn't handle non-finite values.
Results may differ from a plain program's by a relative error of at most 0.0003.
Values sent between devices are 32-bit elements; how exact they have to be, the bound alone decides.
A program may use at most 192 MiB of HBM per device.

v0:
```python
import jax
import jax.numpy as jnp
from jax import lax
from jax.sharding import PartitionSpec as P

HIGH = lax.Precision.HIGHEST


def carried_in(part, axis, combine, identity, reverse):
    count = lax.axis_size(axis)
    place = lax.axis_index(axis)
    ahead = count - 1 - place if reverse else place
    gathered = jax.tree.map(lambda a: lax.all_gather(a, axis), part)
    state = jax.tree.map(lambda a, e: jnp.zeros_like(a) + jnp.asarray(e, a.dtype), part, identity)

    def one(step, state):
        source = count - 1 - step if reverse else step
        return combine(
            state, jax.tree.map(lambda a: lax.dynamic_index_in_dim(a, source, 0, False), gathered)
        )

    return lax.fori_loop(0, ahead, one, state)


def product(left, right):
    return jnp.dot(left, right, precision=HIGH, preferred_element_type=jnp.float32)


def join_maps(earlier, later):
    return (product(earlier[0], later[0]), product(earlier[1], later[0]) + later[1])


def forward_step(state, blocks):
    rhs, coupling, inverse = blocks
    fresh = product(rhs - product(state, coupling), inverse)
    return (fresh, fresh)


def forward_compose_plain(acc, blocks):
    coupling, inverse = blocks
    return (-product(product(acc, coupling), inverse), None)


def backward_step(carry, blocks):
    state, coupling = blocks
    solved = state - carry
    return (product(solved, coupling), solved)


def backward_compose(acc, coupling):
    return (-product(acc, coupling), None)


def on_device(sketch, inv_diag, upper, lower):
    count = sketch.shape[0]
    columns = sketch.shape[1]
    width = sketch.shape[2]
    eye = jnp.eye(width, dtype=jnp.float32)
    blank = jnp.zeros((columns, width), jnp.float32)
    fwd_map, _ = lax.scan(forward_compose_plain, eye, (upper, inv_diag))
    fwd_end, zero_states = lax.scan(forward_step, blank, (sketch, upper, inv_diag))
    incoming = carried_in((fwd_map, fwd_end), "chain", join_maps, (eye, blank), False)[1]
    _, states = lax.scan(forward_step, incoming, (sketch, upper, inv_diag))
    back_map, _ = lax.scan(backward_compose, eye, lower, reverse=True)
    back_end, _ = lax.scan(backward_step, blank, (states, lower), reverse=True)
    from_above = carried_in((back_map, back_end), "chain", join_maps, (eye, blank), True)[1]
    _, solved = lax.scan(backward_step, from_above, (states, lower), reverse=True)
    local_gram = jnp.einsum("skb,slb->kl", solved, solved, precision=HIGH)
    total_gram = lax.psum(local_gram, "chain")
    gram = total_gram / (count * lax.axis_size("chain") * width)
    chol = jnp.linalg.cholesky(gram)
    identity = jnp.eye(columns, dtype=jnp.float32)
    inverse = lax.linalg.triangular_solve(chol, identity, left_side=True, lower=True)
    basis = jnp.einsum("kl,slb->skb", inverse, solved, precision=HIGH)
    return (basis, jnp.transpose(chol))


def solution(mesh):
    placed = (
        P("chain", None, None),
        P("chain", None, None),
        P("chain", None, None),
        P("chain", None, None),
    )
    return jax.shard_map(
        on_device,
        mesh=mesh,
        in_specs=placed,
        out_specs=(P("chain", None, None), P()),
        check_vma=False,
    )
```

profile of v0, /device:TPU:1, one launch (start us, length us, event | category | flops | bytes accessed | tf_op | source)
XLA Modules:
  0.0 677.5 jit_solution(16970784390179098600)
XLA Ops:
  7.2 4.9 while.104
  12.9 6.3 while.103
  12.9 1.5 fusion.96
  14.5 1.6 convolution_negate_fusion.3
  16.0 1.5 fusion.96
  17.6 1.6 convolution_negate_fusion.3
  20.1 3.2 while.102
  20.1 1.6 fusion.91
  21.7 1.6 fusion.91
  24.1 62.6 %all-gather.13.cloned.1.call-done = f32[8192,256]{1,0:T(8,128)} async-done(((f32[64,256]{1,0:T(8,128)}), f32[8192,256]{1,0:T(8,128)}) %all-gather.13.cloned.1.call-update) | async-done | bytes 8388624 | tf_op jit(solution)/shard_map/all_gather | solution.py:13
  86.7 107.3 %all-gather.11.cloned.1.call-done = f32[32768,256]{1,0:T(8,128)} async-done(((f32[256,256]{1,0:T(8,128)}), f32[32768,256]{1,0:T(8,128)}) %all-gather.11.cloned.1.call-update) | async-done | bytes 33554448 | tf_op jit(solution)/shard_map/all_gather | solution.py:13
  194.0 1.2 while.105
  195.3 4.9 while.106
  200.2 2.5 while.107
  203.4 118.0 %all-gather.9.cloned.1.call-done = f32[32768,256]{0,1:T(8,128)} async-done(((f32[256,256]{0,1:T(8,128)}), f32[32768,256]{0,1:T(8,128)}) %all-gather.9.cloned.1.call-update) | async-done | bytes 33554448 | tf_op jit(solution)/shard_map/all_gather | solution.py:13
  321.3 33.4 %copy.7 = f32[32768,256]{1,0:T(8,128)} copy(f32[32768,256]{0,1:T(8,128)} %all-gather.9.cloned.1.call-done) | data formatting | bytes 67108864 | tf_op jit(solution)/shard_map/all_gather | solution.py:13
  354.8 78.0 %all-gather.15.cloned.1.call-done = f32[8192,256]{1,0:T(8,128)} async-done(((f32[64,256]{1,0:T(8,128)}), f32[8192,256]{1,0:T(8,128)}) %all-gather.15.cloned.1.call-update) | async-done | bytes 8388624 | tf_op jit(solution)/shard_map/all_gather | solution.py:13
  432.8 160.3 %while.108 = (s32[]{:T(128)}, f32[64,256]{1,0:T(8,128)S(1)}, s32[]{:T(128)}, f32[128,256,256]{2,1,0:T(8,128)}, f32[128,64,256]{2,1,0:T(8,128)}, /*index=5*/s32[]{:T(128)}, s32[]{:T(128)}, s32[]{:T(128)}, s32[]{:T(128)}) while((s32[]{:T(128)}, f32[64,256]{1,0:T(8,128)S(1)}, s32[]{:T(128)}, f32[128,256,256]{2,1,0:T(8,128)}, ...), condition=%wide.region_13.14_spmd, body=%wide.region_12.13_spmd.sunk | while | flops 50348036 | bytes 590987 | solution.py:22
  451.9 1.2 fusion.114
  472.2 1.2 fusion.114
  492.6 1.2 fusion.114
  594.0 63.0 %psum.7 = f32[64,64]{0,1:T(8,128)S(1)} all-reduce(f32[64,64]{0,1:T(8,128)S(1)} %convolution_bitcast_fusion.6), channel_id=1, replica_groups=mesh['chain'=128] {'chain'}, use_global_device_ids=true, to_apply=%region_16.17 | all-reduce | flops 4096 | bytes 32768 | tf_op jit(solution)/shard_map/psum | solution.py:69
  657.1 5.8 cholesky.17
  664.2 4.9 custom-call.6
  (309 shorter events, 173.2 us)
Async XLA Ops:
  7.2 79.6 %all-gather.13.cloned.1.call-start = ((), (), s32[]{:S(2)}) async-start(), calls=%async_computation.2 | async-start | bytes 8454144 | tf_op jit(solution)/shard_map/all_gather | solution.py:13
  12.1 0.6 copy-start.3
  12.8 181.2 %all-gather.11.cloned.1.call-start = ((), (), s32[]{:S(2)}) async-start(), calls=%async_computation.1 | async-start | bytes 33816576 | tf_op jit(solution)/shard_map/all_gather | solution.py:13
  19.2 0.7 copy-start.2
  19.9 301.4 %all-gather.9.cloned.1.call-start = ((), (), s32[]{:S(2)}) async-start(), calls=%async_computation | async-start | bytes 33816576 | tf_op jit(solution)/shard_map/all_gather | solution.py:13
  23.3 0.7 copy-start.1
  24.0 408.7 %all-gather.15.cloned.1.call-start = ((), (), s32[]{:S(2)}) async-start(), calls=%async_computation.3 | async-start | bytes 8454144 | tf_op jit(solution)/shard_map/all_gather | solution.py:13
  202.7 0.6 copy-start.4
  203.4 389.7 %copy-start = (f32[2,256,256]{2,1,0:T(8,128)S(1)}, f32[2,256,256]{2,1,0:T(8,128)}, u32[]{:S(2)}) copy-start(f32[2,256,256]{2,1,0:T(8,128)} %get-tuple-element.950) | copy-start | bytes 1572868
Sparse Core Ops, SparseCore 0:
  12.9 73.7 all-gather.12
  89.7 104.2 all-gather.10
  196.9 124.4 all-gather.8
  324.7 107.9 all-gather.14
where the time goes:
time: 681 us; the launch traced here: 678 us
  waiting for transfers between devices  366 us (54%)
  matrix products  179 us (26%)
  blocking collectives  63 us (9%)
  local copies, waits for them, and re-layouts  37.9 us (6%)
  between operations  14 us (2%)
  other arithmetic  12.1 us (2%)
    all_gather x4, waiting for transfers between devices, carried_in(): gathered = jax.tree.map(lambda a: lax.all_gather(a, axis), part)  366 us
    dot_general x145, matrix products, product(): jnp.dot(left, right, precision=HIGH, preferred_element_type=jnp.float32)  178 us
    psum x1, blocking collectives, on_device(): total_gram = lax.psum(local_gram, 'chain')  63 us
    all_gather x1, local copies, waits for them, and re-layouts, carried_in(): gathered = jax.tree.map(lambda a: lax.all_gather(a, axis), part)  33.4 us
  transfers between devices with their start and end apart: 4, of which 4 were waited for; matrix products, arithmetic and copies ran while one was open for 8% of the time, Pallas kernels for 0%

commit v1 on v0

--- a/solution.py
+++ b/solution.py
@@ -66,7 +66,7 @@
     from_above = carried_in((back_map, back_end), "chain", join_maps, (eye, blank), True)[1]
     _, solved = lax.scan(backward_step, from_above, (states, lower), reverse=True)
     local_gram = jnp.einsum("skb,slb->kl", solved, solved, precision=HIGH)
-    total_gram = lax.psum(local_gram, "chain")
+    total_gram = jnp.sum(lax.all_gather(local_gram, "chain"), axis=0)
     gram = total_gram / (count * lax.axis_size("chain") * width)
     chol = jnp.linalg.cholesky(gram)
     identity = jnp.eye(columns, dtype=jnp.float32)

time: 681 us -> 683 us (level)
  blocking collectives: 63 us -> 0 us
  waiting for transfers between devices: 366 us -> 428 us
    psum x1 -> x0, blocking collectives: 63 us -> none  [on_device(): total_gram = lax.psum(local_gram, 'chain')]
    all_gather x0 -> x1, waiting for transfers between devices: none -> 61.7 us  [on_device(): total_gram = jnp.sum(lax.all_gather(local_gram, 'chain'), axis=0)]
  transfers between devices with their start and end apart: 4 -> 5, of which waited for: 4 -> 5; matrix products, arithmetic and copies ran while one was open for 8% -> 8% of each run, Pallas kernels for 0% -> 0%
where the time goes in v1:
time: 683 us; the launch traced here: 679 us
  waiting for transfers between devices  428 us (63%)
  matrix products  180 us (26%)
  local copies, waits for them, and re-layouts  38 us (6%)
  other arithmetic  14.7 us (2%)
  between operations  14 us (2%)
    all_gather x4, waiting for transfers between devices, carried_in(): gathered = jax.tree.map(lambda a: lax.all_gather(a, axis), part)  366 us
    dot_general x145, matrix products, product(): jnp.dot(left, right, precision=HIGH, preferred_element_type=jnp.float32)  178 us
    all_gather x1, waiting for transfers between devices, on_device(): total_gram = jnp.sum(lax.all_gather(local_gram, 'chain'), axis=0)  61.7 us
    all_gather x1, local copies, waits for them, and re-layouts, carried_in(): gathered = jax.tree.map(lambda a: lax.all_gather(a, axis), part)  33.4 us
  transfers between devices with their start and end apart: 5, of which 5 were waited for; matrix products, arithmetic and copies ran while one was open for 8% of the time, Pallas kernels for 0%

profile of v1, /device:TPU:1, one launch (start us, length us, event | category | flops | bytes accessed | tf_op | source)
XLA Modules:
  0.0 679.4 jit_solution(2427318953406942483)
XLA Ops:
  7.2 4.9 while.104
  12.9 6.3 while.103
  12.9 1.5 fusion.96
  14.5 1.6 convolution_negate_fusion.3
  16.0 1.5 fusion.96
  17.6 1.6 convolution_negate_fusion.3
  20.1 3.2 while.102
  20.1 1.6 fusion.91
  21.7 1.6 fusion.91
  24.1 62.6 %all-gather.15.cloned.1.call-done = f32[8192,256]{1,0:T(8,128)} async-done(((f32[64,256]{1,0:T(8,128)}), f32[8192,256]{1,0:T(8,128)}) %all-gather.15.cloned.1.call-update) | async-done | bytes 8388624 | tf_op jit(solution)/shard_map/all_gather | solution.py:13
  86.7 107.3 %all-gather.13.cloned.1.call-done = f32[32768,256]{1,0:T(8,128)} async-done(((f32[256,256]{1,0:T(8,128)}), f32[32768,256]{1,0:T(8,128)}) %all-gather.13.cloned.1.call-update) | async-done | bytes 33554448 | tf_op jit(solution)/shard_map/all_gather | solution.py:13
  194.0 1.2 while.105
  195.3 4.9 while.106
  200.2 2.5 while.107
  203.4 117.9 %all-gather.11.cloned.1.call-done = f32[32768,256]{0,1:T(8,128)} async-done(((f32[256,256]{0,1:T(8,128)}), f32[32768,256]{0,1:T(8,128)}) %all-gather.11.cloned.1.call-update) | async-done | bytes 33554448 | tf_op jit(solution)/shard_map/all_gather | solution.py:13
  321.3 33.4 %copy.11 = f32[32768,256]{1,0:T(8,128)} copy(f32[32768,256]{0,1:T(8,128)} %all-gather.11.cloned.1.call-done) | data formatting | bytes 67108864 | tf_op jit(solution)/shard_map/all_gather | solution.py:13
  354.8 78.0 %all-gather.17.cloned.1.call-done = f32[8192,256]{1,0:T(8,128)} async-done(((f32[64,256]{1,0:T(8,128)}), f32[8192,256]{1,0:T(8,128)}) %all-gather.17.cloned.1.call-update) | async-done | bytes 8388624 | tf_op jit(solution)/shard_map/all_gather | solution.py:13
  432.8 160.3 %while.108 = (s32[]{:T(128)}, f32[64,256]{1,0:T(8,128)S(1)}, s32[]{:T(128)}, f32[128,256,256]{2,1,0:T(8,128)}, f32[128,64,256]{2,1,0:T(8,128)}, /*index=5*/s32[]{:T(128)}, s32[]{:T(128)}, s32[]{:T(128)}, s32[]{:T(128)}) while((s32[]{:T(128)}, f32[64,256]{1,0:T(8,128)S(1)}, s32[]{:T(128)}, f32[128,256,256]{2,1,0:T(8,128)}, ...), condition=%wide.region_13.14_spmd, body=%wide.region_12.13_spmd.sunk | while | flops 50348036 | bytes 590987 | solution.py:22
  443.0 1.2 fusion.114
  463.3 1.2 fusion.114
  594.6 61.7 %all-gather.19.cloned.1.call-done = f32[8192,64]{1,0:T(8,128)} async-done(((f32[64,64]{1,0:T(8,128)}), f32[8192,64]{1,0:T(8,128)}) %all-gather.19.cloned.1.call-update) | async-done | bytes 2097168 | tf_op jit(solution)/shard_map/all_gather | solution.py:69
  656.3 2.5 reduce_sum.11
  658.9 5.8 cholesky.17
  666.1 4.9 custom-call.6
  (311 shorter events, 175.1 us)
Async XLA Ops:
  7.2 79.6 %all-gather.15.cloned.1.call-start = ((), (), s32[]{:S(2)}) async-start(), calls=%async_computation.2 | async-start | bytes 8454144 | tf_op jit(solution)/shard_map/all_gather | solution.py:13
  12.1 0.6 copy-start.3
  12.8 181.2 %all-gather.13.cloned.1.call-start = ((), (), s32[]{:S(2)}) async-start(), calls=%async_computation.1 | async-start | bytes 33816576 | tf_op jit(solution)/shard_map/all_gather | solution.py:13
  19.2 0.7 copy-start.2
  19.9 301.4 %all-gather.11.cloned.1.call-start = ((), (), s32[]{:S(2)}) async-start(), calls=%async_computation | async-start | bytes 33816576 | tf_op jit(solution)/shard_map/all_gather | solution.py:13
  23.3 0.7 copy-start.1
  24.1 408.7 %all-gather.17.cloned.1.call-start = ((), (), s32[]{:S(2)}) async-start(), calls=%async_computation.3 | async-start | bytes 8454144 | tf_op jit(solution)/shard_map/all_gather | solution.py:13
  202.7 0.6 copy-start.4
  203.4 452.9 %all-gather.19.cloned.1.call-start = ((), (), s32[]{:S(2)}) async-start(), calls=%async_computation.4 | async-start | bytes 4227072 | tf_op jit(solution)/shard_map/all_gather | solution.py:69
  203.4 389.7 %copy-start = (f32[2,256,256]{2,1,0:T(8,128)S(1)}, f32[2,256,256]{2,1,0:T(8,128)}, u32[]{:S(2)}) copy-start(f32[2,256,256]{2,1,0:T(8,128)} %get-tuple-element.956) | copy-start | bytes 1572868
Sparse Core Ops, SparseCore 0:
  12.9 73.7 all-gather.14
  89.7 104.2 all-gather.12
  196.9 124.4 all-gather.10
  324.7 107.9 all-gather.16
  594.8 61.4 all-gather.18
